TPU v7x, 128 devices: a whole 4x4x4 slice. The times are simulated.
128 devices in a mesh: vc: 8 (over x, core), vd: 16 (over z, y).
Axes of the slice: x: 4, y: 4, z: 4, core: 2. Of those that a mesh axis runs over, the one named last changes fastest.
Arguments:
- integrals: bfloat16 [2048, 262144], P(('vc', 'vd')), may hold values from -0.015625 to 0.015625
- amplitudes: bfloat16 [2048, 262144], P(('vc', 'vd')), may hold values from -6 to 6
- block_lists: int32 [128, 15], replicated, may hold values from -1 to 2047, as said below
Outputs:
- ladder: float32 [2048, 2048], P(('vc', 'vd'))
Inputs may be any that keep to these rules, and one draw needn't show every extreme that they name: `block_lists`: row r lists in its first slots the screened blocks of device r (index along vc+vd), then -1 in the rest; no block appears twice in the whole array; each row holds 1 to 15 blocks and some row exactly 15; exactly 1024 entries are blocks.
All inputs are finite; a program needn't handle non-finite values.
Results may differ from a plain program's by a relative error of at most 0.0003.
Values may be sent and summed in bfloat16 or wider, within the bound.
A program may use at most 128 MiB of HBM per device.

v0:
```python
import jax
import jax.numpy as jnp
from jax import lax
from jax.sharding import PartitionSpec as P

BW = 128
MOSTB = 15


def pack_blocks(local_rows, owner_table, count_all, slot_count):
    row_count = local_rows.shape[0]
    block_count = local_rows.shape[1] // BW
    by_block = local_rows.reshape(row_count, block_count, BW)
    flat_owner = owner_table.reshape(-1)
    safe_ids = jnp.maximum(flat_owner, 0)
    picked = jnp.take(by_block, safe_ids, axis=1)
    keep_mask = (flat_owner >= 0)[None, :, None]
    picked = jnp.where(keep_mask, picked, jnp.zeros_like(picked))
    picked = picked.reshape(row_count, count_all, slot_count, BW)
    return jnp.moveaxis(picked, 1, 0)


def shards(integrals, amplitudes, block_lists):
    count_all = lax.axis_size(("vc", "vd"))
    rows_int = integrals.shape[0]
    rows_amp = amplitudes.shape[0]
    slot_count = MOSTB
    send_int = pack_blocks(integrals, block_lists, count_all, slot_count)
    send_amp = pack_blocks(amplitudes, block_lists, count_all, slot_count)
    got_int, got_amp = (
        lax.all_to_all(send_int, ("vc", "vd"), split_axis=0, concat_axis=0, tiled=True),
        lax.all_to_all(send_amp, ("vc", "vd"), split_axis=0, concat_axis=0, tiled=True),
    )
    owned_int = got_int.reshape(count_all * rows_int, slot_count * BW)
    owned_amp = got_amp.reshape(count_all * rows_amp, slot_count * BW)
    return lax.psum_scatter(
        lax.dot_general(
            owned_amp, owned_int, (((1,), (1,)), ((), ())), preferred_element_type=jnp.float32
        ),
        ("vc", "vd"),
        scatter_dimension=0,
        tiled=True,
    )


def solution(mesh):
    return jax.shard_map(
        shards,
        mesh=mesh,
        in_specs=(P(("vc", "vd"), None), P(("vc", "vd"), None), P()),
        out_specs=P(("vc", "vd"), None),
        check_vma=False,
    )
```

profile of v0, /device:TPU:0, one launch (start us, length us, event | category | flops | bytes accessed | tf_op | source)
XLA Modules:
  0.0 971.6 jit_solution(9677025383865186912)
XLA Ops:
  6.5 0.7 broadcast_compare_fusion
  7.2 0.7 broadcast_maximum_fusion
  7.9 0.1 copy.9
  8.0 0.2 max.8
  8.3 0.1 copy.8
  8.4 0.2 ge.17
  8.6 0.0 copy-start
  8.7 7.9 copy_bitcast_fusion
  16.6 1.0 copy-done
  17.6 4.0 copy_bitcast_fusion.1
  21.6 10.2 %gather_fusion.1 = bf16[1920,16,128]{2,1,0:T(8,128)(2,1)} fusion(bf16[16,2048,128]{2,0,1:T(8,128)(2,1)} %copy_bitcast_fusion, s32[2048]{0:T(1024)S(1)} %pad_clamp_fusion), kind=kCustom, calls=%fused_computation.1.clone | custom fusion | bytes 15736320 | tf_op jit(solution)/shard_map/jit(_take)/gather | solution.py:16
  31.8 10.3 %gather_fusion = bf16[1920,16,128]{2,1,0:T(8,128)(2,1)} fusion(bf16[16,2048,128]{2,0,1:T(8,128)(2,1)} %copy_bitcast_fusion.1, s32[2048]{0:T(1024)S(1)} %pad_clamp_fusion), kind=kCustom, calls=%fused_computation.clone | custom fusion | bytes 15736320 | tf_op jit(solution)/shard_map/jit(_take)/gather | solution.py:16
  42.1 12.6 %bitcast_select_fusion.1 = (bf16[16,1920,128]{2,0,1:T(8,128)(2,1)S(1)}, bf16[16,1920,128]{2,0,1:T(8,128)(2,1)}) fusion(bf16[1920,16,128]{2,1,0:T(8,128)(2,1)} %gather_fusion, pred[1920]{0:T(1024)(128)(4,1)S(1)} %compare_and_fusion, pred[1920]{0:T(1024)(128)(4,1)S(1)} %ge.17, bf16[1920,16,128]{2,1,0:T(8,128)(2,1)} %gather_fusion.1), kind=kLoop, calls=%fused_computation.10 | loop fusion | flops 15728640 | bytes 31461120 | tf_op jit(solution)/shard_map/jit(_where)/select_n | solution.py:18
  54.7 102.3 %all_to_all.10 = bf16[128,16,15,128]{3,1,2,0:T(8,128)(2,1)} all-to-all(bf16[128,16,15,128]{3,1,2,0:T(8,128)(2,1)S(1)} %bitcast.31), channel_id=1, replica_groups=mesh['vc'=8,'vd'=16] {'vc','vd'}, dimensions={0} | all-to-all | bytes 15728640 | tf_op jit(solution)/shard_map/all_to_all | solution.py:32
  157.0 6.7 all-to-all-start.1
  163.6 0.2 reduce-scatter.2.cloned.1.call-start
  163.9 10.7 %copy.11 = bf16[128,16,15,128]{3,2,1,0:T(8,128)(2,1)} copy(bf16[128,16,15,128]{3,1,2,0:T(8,128)(2,1)} %all_to_all.10) | data formatting | bytes 15728640 | tf_op jit(solution)/shard_map/all_to_all | solution.py:32
  174.5 88.2 %all-to-all-done.1 = bf16[128,16,15,128]{3,1,2,0:T(8,128)(2,1)} async-done(((bf16[128,16,15,128]{3,1,2,0:T(8,128)(2,1)}), bf16[128,16,15,128]{3,1,2,0:T(8,128)(2,1)}, u32[]{:S(2)}, u32[]{:S(2)}) %all-to-all-start.1) | async-done | bytes 7864352 | tf_op jit(solution)/shard_map/all_to_all | solution.py:31
  262.7 10.7 %copy.13 = bf16[128,16,15,128]{3,2,1,0:T(8,128)(2,1)} copy(bf16[128,16,15,128]{3,1,2,0:T(8,128)(2,1)} %all-to-all-done.1) | data formatting | bytes 15728640 | tf_op jit(solution)/shard_map/all_to_all | solution.py:31
  273.4 24.6 %fusion = f32[2048,2048]{1,0:T(8,128)} fusion(bf16[256,8,15,128]{3,2,1,0:T(8,128)(2,1)} %bitcast.33, bf16[256,8,15,128]{3,2,1,0:T(8,128)(2,1)} %bitcast.32), kind=kOutput, calls=%fused_computation.4 | convolution fusion | flops 16106127360 | bytes 32505856 | tf_op jit(solution)/shard_map/dot_general | solution.py:37
  297.9 0.0 reduce-scatter.2.cloned.1.call-update
  298.0 666.8 %reduce-scatter.2.cloned.1.call-done = f32[16,2048]{1,0:T(8,128)} async-done(((f32[2048,2048]{1,0:T(8,128)}), f32[16,2048]{1,0:T(8,128)}) %reduce-scatter.2.cloned.1.call-update) | async-done | bytes 131088 | tf_op jit(solution)/shard_map/reduce_scatter | solution.py:36
  (3 shorter events, 0.0 us)
Async XLA Ops:
  8.6 8.9 copy-start
  157.0 105.8 %all-to-all-start.1 = ((bf16[128,16,15,128]{3,1,2,0:T(8,128)(2,1)}), bf16[128,16,15,128]{3,1,2,0:T(8,128)(2,1)}, u32[]{:S(2)}, u32[]{:S(2)}) async-start(bf16[128,16,15,128]{3,1,2,0:T(8,128)(2,1)} %bitcast.30), calls=%async_computation.1 | async-start | bytes 15728640 | tf_op jit(solution)/shard_map/all_to_all | solution.py:31
  163.6 801.1 %reduce-scatter.2.cloned.1.call-start = ((), (), s32[]{:S(2)}) async-start(), calls=%async_computation.3 | async-start | bytes 16908288 | tf_op jit(solution)/shard_map/reduce_scatter | solution.py:36
Sparse Core Ops, SparseCore 0:
  298.1 666.6 reduce-scatter.1
where the time goes:
time: 972 us
  waiting for transfers between devices  755 us (78%)
  blocking collectives  102 us (10%)
  local copies, waits for them, and re-layouts  55.4 us (6%)
  matrix products  24.6 us (3%)
  other arithmetic  14 us (1%)
  between operations  13.5 us (1%)
    reduce_scatter x1, waiting for transfers between devices, shards(): lax.psum_scatter(lax.dot_general(owned_amp, owned_int, (((1,), (1,)), (()...  667 us
    all_to_all x1, blocking collectives, shards(): lax.all_to_all(send_amp, ('vc', 'vd'), split_axis=0, concat_axis=0, tiled...  102 us
    all_to_all x1, waiting for transfers between devices, shards(): lax.all_to_all(send_int, ('vc', 'vd'), split_axis=0, concat_axis=0, tiled...  88.2 us
    dot_general x1, matrix products, shards(): lax.dot_general(owned_amp, owned_int, (((1,), (1,)), ((), ())), preferred...  24.6 us
    gather x2, local copies, waits for them, and re-layouts, pack_blocks(): picked = jnp.take(by_block, safe_ids, axis=1)  20.5 us
  transfers between devices with their start and end apart: 2, of which 2 were waited for; matrix products, arithmetic and copies ran while one was open for 1% of the time, Pallas kernels for 0%

commit v1 on v0

v1 whole, which is shorter than its diff:
```python
import functools
import random

import jax
import jax.numpy as jnp
from jax import lax
from jax.experimental import pallas as pl
from jax.experimental.pallas import tpu as pltpu
from jax.sharding import PartitionSpec as P

MESH = pl.DeviceIdType.MESH
BW = 128
NX, NC, NY, NZ = 4, 2, 4, 4
GROUP = NX * NC * NY
LISTED = 1024
MIB = 1 << 20


def plane_index(x, c, y):
    return (x * NC + c) * NY + y


def device(x, c, y, z):
    return (x * NC + c, z * NY + y)


def wait_bytes(ref, sem):
    pltpu.make_async_copy(ref, ref, sem).wait()


def list_blocks(lists, ids):
    slots = lists.shape[1]

    def one(row, filled):
        used = jnp.int32(0)
        for slot in range(slots):
            block = lists[row, slot]
            ids[filled + slot] = block
            used += (block >= 0).astype(jnp.int32)
        return filled + used

    lax.fori_loop(0, lists.shape[0], one, jnp.int32(0))


def kernel(
    steps, ahead, ids, amp_hbm, int_hbm, out_ref,
    amp, integ, packed, own, amp_z, int_z, total, half, part_x, part_y, sum_x, sum_y, end_y, end_x, done, other,
    load_sem, send_sem, recv_sem, zsend_sem, zrecv_sem, rsend_sem, rrecv_sem,
):
    vc, vd = lax.axis_index("vc"), lax.axis_index("vd")
    x, c, z, y = vc // NC, lax.rem(vc, NC), vd // NY, lax.rem(vd, NY)
    me = plane_index(x, c, y)
    amp_peer = device(x, c, y, 3 - z)
    int_peer = device(x, c, y, z + 1 - 2 * lax.rem(z, 2))
    order = [(dx, dc, dy) for dx in range(NX) for dc in range(NC) for dy in range(NY)][1:]
    random.Random(2).shuffle(order)
    peers = []
    for dx, dc, dy in order:
        px, pc, py = lax.rem(x + dx, NX), lax.rem(c + dc, NC), lax.rem(y + dy, NY)
        peers.append((plane_index(px, pc, py), device(px, pc, py, z)))
    columns = packed.shape[3]
    blocks = columns // BW

    loads = [
        pltpu.make_async_copy(amp_hbm, amp, load_sem.at[0]),
        pltpu.make_async_copy(int_hbm, integ, load_sem.at[1]),
    ]
    for load in loads:
        load.start()
    barrier = pltpu.get_barrier_semaphore()
    everyone = [place for _, place in peers] + [amp_peer, int_peer]
    for place in everyone:
        pl.semaphore_signal(barrier, inc=1, device_id=place, device_id_type=MESH)
    total[...] = jnp.zeros_like(total)
    for load in loads:
        load.wait()

    def pack(step):
        def one(member, carry):
            for block in range(blocks):
                start = ids[(step * GROUP + member) * blocks + block] * BW
                packed[step, member, 0:16, block * BW:(block + 1) * BW] = amp[:, pl.ds(start, BW)]
                packed[step, member, 16:32, block * BW:(block + 1) * BW] = integ[:, pl.ds(start, BW)]
            return carry

        lax.fori_loop(0, GROUP, one, 0)

    def send(step):
        for index, place in peers:
            pltpu.make_async_remote_copy(
                src_ref=packed.at[step, index], dst_ref=own.at[step, me],
                send_sem=send_sem, recv_sem=recv_sem.at[step], device_id=place, device_id_type=MESH,
            ).start()
        pltpu.make_async_copy(packed.at[step, me], own.at[step, me], recv_sem.at[step]).start()

    def pass_on(step):
        wait_bytes(own.at[step], recv_sem.at[step])
        pltpu.make_async_remote_copy(
            src_ref=own.at[step, :, 0:16, :], dst_ref=amp_z.at[step],
            send_sem=zsend_sem, recv_sem=zrecv_sem.at[0, step], device_id=amp_peer, device_id_type=MESH,
        ).start()
        pltpu.make_async_remote_copy(
            src_ref=own.at[step, :, 16:32, :], dst_ref=int_z.at[step],
            send_sem=zsend_sem, recv_sem=zrecv_sem.at[1, step], device_id=int_peer, device_id_type=MESH,
        ).start()

    def multiply(step):
        wait_bytes(amp_z.at[step], zrecv_sem.at[0, step])
        wait_bytes(int_z.at[step], zrecv_sem.at[1, step])
        rows = GROUP * 16
        lhs = [own[step, :, 0:16, :].reshape(rows, columns), amp_z[step].reshape(rows, columns)]
        for n in range(4):
            pieces = []
            for xc in (2 * n, 2 * n + 1):
                pieces.append(own[step, NY * xc:NY * (xc + 1), 16:32, :].reshape(64, columns))
                pieces.append(int_z[step, NY * xc:NY * (xc + 1)].reshape(64, columns))
            rhs = jnp.concatenate(pieces, axis=0)
            for which in range(2):
                term = lax.dot_general(lhs[which], rhs, (((1,), (1,)), ((), ())), preferred_element_type=jnp.float32)
                total[n, which] += term.reshape(NX, NC, NY, 16, 256)

    pack(0)
    pl.semaphore_wait(barrier, len(everyone))
    send(0)
    for step in range(1, ahead):
        pack(step)
        send(step)

    def turn(step, carry):
        pack(step + ahead)
        send(step + ahead)
        pass_on(step)

        @pl.when(step > 0)
        def _():
            multiply(step - 1)

        return carry

    lax.fori_loop(0, steps - ahead, turn, 0)

    def last(step, carry):
        pass_on(step)
        multiply(step - 1)
        return carry

    lax.fori_loop(steps - ahead, steps, last, 0)
    multiply(steps - 1)

    copy = pltpu.make_async_remote_copy(
        src_ref=total.at[:, :, :, 1 - c], dst_ref=half, send_sem=rsend_sem.at[0], recv_sem=rrecv_sem.at[0],
        device_id=device(x, 1 - c, y, z), device_id_type=MESH,
    )
    copy.start()
    copy.wait()
    half[...] += total[:, :, :, c]

    copies = []
    for d in (1, 2, 3):
        px, py = lax.rem(x + d, NX), lax.rem(y + d, NY)
        copies.append(pltpu.make_async_remote_copy(
            src_ref=half.at[0:2, :, px], dst_ref=part_x.at[d - 1], send_sem=rsend_sem.at[d], recv_sem=rrecv_sem.at[d],
            device_id=device(px, c, y, z), device_id_type=MESH,
        ))
        copies.append(pltpu.make_async_remote_copy(
            src_ref=half.at[2:4, :, :, py], dst_ref=part_y.at[d - 1], send_sem=rsend_sem.at[3 + d], recv_sem=rrecv_sem.at[3 + d],
            device_id=device(x, c, py, z), device_id_type=MESH,
        ))
    for copy in copies:
        copy.start()
    for copy in copies:
        copy.wait()
    sum_x[...] = half[0:2, :, x] + part_x[0] + part_x[1] + part_x[2]
    sum_y[...] = half[2:4, :, :, y] + part_y[0] + part_y[1] + part_y[2]

    copies = []
    for d in (1, 2, 3):
        px, py = lax.rem(x + d, NX), lax.rem(y + d, NY)
        copies.append(pltpu.make_async_remote_copy(
            src_ref=sum_x.at[:, :, py], dst_ref=end_y.at[d - 1], send_sem=rsend_sem.at[6 + d], recv_sem=rrecv_sem.at[6 + d],
            device_id=device(x, c, py, z), device_id_type=MESH,
        ))
        copies.append(pltpu.make_async_remote_copy(
            src_ref=sum_y.at[:, :, px], dst_ref=end_x.at[d - 1], send_sem=rsend_sem.at[9 + d], recv_sem=rrecv_sem.at[9 + d],
            device_id=device(px, c, y, z), device_id_type=MESH,
        ))
    for copy in copies:
        copy.start()
    for copy in copies:
        copy.wait()
    done[0:2] = sum_x[:, :, y] + end_y[0] + end_y[1] + end_y[2]
    done[2:4] = sum_y[:, :, x] + end_x[0] + end_x[1] + end_x[2]

    copy = pltpu.make_async_remote_copy(
        src_ref=done.at[:, 1], dst_ref=other, send_sem=rsend_sem.at[13], recv_sem=rrecv_sem.at[13],
        device_id=amp_peer, device_id_type=MESH,
    )
    copy.start()
    odd, high = lax.rem(z, 2), z // 2

    def place(values, n, swap, upper):
        for j in range(2):
            piece = values[:, j * BW:(j + 1) * BW]
            piece = jnp.where(swap == 1, pltpu.roll(piece, BW // 2, 1), piece)
            start = pl.multiple_of((2 * n + j) * 2 * BW + upper * BW, BW)
            out_ref[:, pl.ds(start, BW)] = piece

    for n in range(4):
        place(done[n, 0], n, odd, high)
    copy.wait()
    for n in range(4):
        place(other[n], n, 1 - odd, 1 - high)

    for _ in range(steps):
        wait_bytes(packed.at[0, 0:GROUP - 1], send_sem)
        wait_bytes(own.at[0], zsend_sem)


def solution(mesh):
    steps, ahead = 16, 2

    def shards(integrals, amplitudes, block_lists):
        columns = LISTED * BW // GROUP // steps
        f32, bf16 = jnp.float32, jnp.bfloat16
        ids = pl.pallas_call(
            list_blocks,
            out_shape=jax.ShapeDtypeStruct((LISTED + 16,), jnp.int32),
            in_specs=[pl.BlockSpec(memory_space=pltpu.SMEM)],
            out_specs=pl.BlockSpec(memory_space=pltpu.SMEM),
            name="list_blocks",
        )(block_lists)
        return pl.pallas_call(
            functools.partial(kernel, steps, ahead),
            out_shape=jax.ShapeDtypeStruct((16, 2048), f32),
            in_specs=[
                pl.BlockSpec(memory_space=pltpu.SMEM),
                pl.BlockSpec(memory_space=pl.ANY),
                pl.BlockSpec(memory_space=pl.ANY),
            ],
            out_specs=pl.BlockSpec(memory_space=pltpu.VMEM),
            scratch_shapes=[
                pltpu.VMEM(amplitudes.shape, bf16),
                pltpu.VMEM(integrals.shape, bf16),
                pltpu.VMEM((steps, GROUP, 32, columns), bf16),
                pltpu.VMEM((steps, GROUP, 32, columns), bf16),
                pltpu.VMEM((steps, GROUP, 16, columns), bf16),
                pltpu.VMEM((steps, GROUP, 16, columns), bf16),
                pltpu.VMEM((4, 2, NX, NC, NY, 16, 256), f32),
                pltpu.VMEM((4, 2, NX, NY, 16, 256), f32),
                pltpu.VMEM((3, 2, 2, NY, 16, 256), f32),
                pltpu.VMEM((3, 2, 2, NX, 16, 256), f32),
                pltpu.VMEM((2, 2, NY, 16, 256), f32),
                pltpu.VMEM((2, 2, NX, 16, 256), f32),
                pltpu.VMEM((3, 2, 2, 16, 256), f32),
                pltpu.VMEM((3, 2, 2, 16, 256), f32),
                pltpu.VMEM((4, 2, 16, 256), f32),
                pltpu.VMEM((4, 16, 256), f32),
                pltpu.SemaphoreType.DMA((2,)),
                pltpu.SemaphoreType.DMA,
                pltpu.SemaphoreType.DMA((steps,)),
                pltpu.SemaphoreType.DMA,
                pltpu.SemaphoreType.DMA((2, steps)),
                pltpu.SemaphoreType.DMA((14,)),
                pltpu.SemaphoreType.DMA((14,)),
            ],
            compiler_params=pltpu.CompilerParams(
                collective_id=0, has_side_effects=True, vmem_limit_bytes=62 * MIB
            ),
            name="ladder",
        )(ids, amplitudes, integrals)

    return jax.shard_map(
        shards,
        mesh=mesh,
        in_specs=(P(("vc", "vd"), None), P(("vc", "vd"), None), P()),
        out_specs=P(("vc", "vd"), None),
        check_vma=False,
    )
```

time: 972 us -> 153 us (0.16)
  waiting for transfers between devices: 755 us -> 0 us
  Pallas kernels: 0 us -> 149 us
  blocking collectives: 102 us -> 0 us
  local copies, waits for them, and re-layouts: 55.4 us -> 3 us
  matrix products: 24.6 us -> 0 us
  other arithmetic: 14 us -> 0 us
  between operations: 13.5 us -> 0.02 us
    reduce_scatter x1 -> x0, waiting for transfers between devices: 667 us -> none  [shards(): lax.psum_scatter(lax.dot_general(owned_amp, owned_int, (((1,), (1,)), (()...]
    pallas_call x0 -> x2, Pallas kernels: none -> 149 us  [the longest x1 142 us: shards(): pl.pallas_call(functools.partial(kernel, steps, ahead), out_shape=jax.Sha...]
    all_to_all x1 -> x0, blocking collectives: 102 us -> none  [shards(): lax.all_to_all(send_amp, ('vc', 'vd'), split_axis=0, concat_axis=0, tiled...]
    all_to_all x1 -> x0, waiting for transfers between devices: 88.2 us -> none  [shards(): lax.all_to_all(send_int, ('vc', 'vd'), split_axis=0, concat_axis=0, tiled...]
    dot_general x1 -> x0, matrix products: 24.6 us -> none  [shards(): lax.dot_general(owned_amp, owned_int, (((1,), (1,)), ((), ())), preferred...]
    all_to_all x2 -> x0, local copies, waits for them, and re-layouts: 21.3 us -> none  [the longest x1 10.7 us: shards(): lax.all_to_all(send_amp, ('vc', 'vd'), split_axis=0, concat_axis=0, tiled...]
    gather x2 -> x0, local copies, waits for them, and re-layouts: 20.5 us -> none  [pack_blocks(): picked = jnp.take(by_block, safe_ids, axis=1)]
    select_n x2 -> x0, other arithmetic: 12.6 us -> none  [the longest x1 12.6 us: pack_blocks(): picked = jnp.where(keep_mask, picked, jnp.zeros_like(picked))]
  transfers between devices with their start and end apart: 2 -> 0, of which waited for: 2 -> 0; matrix products, arithmetic and copies ran while one was open for 1% -> 0% of each run, Pallas kernels for 0% -> 0%
where the time goes in v1:
time: 153 us; the launch traced here: 152 us
  Pallas kernels  149 us (97%)
  local copies, waits for them, and re-layouts  3 us (2%)
    pallas_call x1, Pallas kernels, shards(): pl.pallas_call(functools.partial(kernel, steps, ahead), out_shape=jax.Sha...  142 us
    pallas_call x1, Pallas kernels, shards(): pl.pallas_call(list_blocks, out_shape=jax.ShapeDtypeStruct((LISTED + 16,)...  6.84 us

profile of v1, /device:TPU:0, one launch (start us, length us, event | category | flops | bytes accessed | tf_op | source)
XLA Modules:
  0.0 152.3 jit_solution(10254882618903262369)
XLA Ops:
  0.0 1.4 copy.4.lists
  1.4 6.8 %list_blocks.1.ids = s32[1040]{0:T(1024)} custom-call(s32[128,15]{1,0:T(8,128)} %copy.4.lists), custom_call_target="tpu_custom_call" | custom-call | tf_op jit(solution)/shard_map/list_blocks/pallas_call | solution.py:225
  8.3 142.5 %ladder.1 = f32[16,2048]{1,0:T(8,128)} custom-call(s32[1040]{0:T(1024)} %list_blocks.1.ids, bf16[16,262144]{1,0:T(8,128)(2,1)} %amp_hbm.1, bf16[16,262144]{1,0:T(8,128)(2,1)} %int_hbm.1), custom_call_target="tpu_custom_call" | custom-call | tf_op jit(solution)/shard_map/ladder/pallas_call | solution.py:232
  150.8 1.6 %copy.6 = f32[16,2048]{1,0:T(8,128)} copy(f32[16,2048]{1,0:T(8,128)} %ladder.1) | data formatting | bytes 262144

commit v2 on v1

v2 whole, which is shorter than its diff:
```python
import functools
import random

import jax
import jax.numpy as jnp
from jax import lax
from jax.experimental import pallas as pl
from jax.experimental.pallas import tpu as pltpu
from jax.sharding import PartitionSpec as P

MESH = pl.DeviceIdType.MESH
BW = 128
NX, NC, NY, NZ = 4, 2, 4, 4
GROUP = NX * NY
LISTED = 1024
MIB = 1 << 20


def device(x, c, y, z):
    return (x * NC + c, z * NY + y)


def wait_bytes(ref, sem):
    pltpu.make_async_copy(ref, ref, sem).wait()


def kernel(
    steps, ahead, lists, amp_hbm, int_hbm, out_ref,
    amp, integ, packed, own, amp_z, int_z, near, total, part_x, part_y, sum_x, sum_y, end_y, end_x, done, other,
    load_sem, send_sem, recv_sem, zsend_sem, zrecv_sem, nsend_sem, nrecv_sem, rsend_sem, rrecv_sem, last_sem,
):
    vc, vd = lax.axis_index("vc"), lax.axis_index("vd")
    x, c, z, y = vc // NC, lax.rem(vc, NC), vd // NY, lax.rem(vd, NY)
    me = x * NY + y
    amp_peer = device(x, c, y, 3 - z)
    int_peer = device(x, c, y, z + 1 - 2 * lax.rem(z, 2))
    near_peer = device(x, 1 - c, y, z)
    order = [(dx, dy) for dx in range(NX) for dy in range(NY)][1:]
    random.Random(1).shuffle(order)
    peers = []
    for dx, dy in order:
        px, py = lax.rem(x + dx, NX), lax.rem(y + dy, NY)
        peers.append((px * NY + py, device(px, c, py, z)))
    columns = packed.shape[3]
    blocks = columns // BW
    slots, owners = lists.shape

    loads = [
        pltpu.make_async_copy(amp_hbm, amp, load_sem.at[0]),
        pltpu.make_async_copy(int_hbm, integ, load_sem.at[1]),
    ]
    for load in loads:
        load.start()
    barrier = pltpu.get_barrier_semaphore()
    everyone = [place for _, place in peers] + [amp_peer, int_peer, near_peer]
    for place in everyone:
        pl.semaphore_signal(barrier, inc=1, device_id=place, device_id_type=MESH)
    total[...] = jnp.zeros_like(total)
    for load in loads:
        load.wait()

    def pack(step, state):
        def one(member, state):
            owner, slot = state
            for block in range(blocks):
                start = lists[slot, owner] * BW
                packed[step, member, 0:16, block * BW:(block + 1) * BW] = amp[:, pl.ds(start, BW)]
                packed[step, member, 16:32, block * BW:(block + 1) * BW] = integ[:, pl.ds(start, BW)]
                following = lists[jnp.minimum(slot + 1, slots - 1), owner]
                stays = jnp.logical_and(slot + 1 < slots, following >= 0)
                slot = jnp.where(stays, slot + 1, 0)
                owner = jnp.minimum(jnp.where(stays, owner, owner + 1), owners - 1)
            return owner, slot

        return lax.fori_loop(0, GROUP, one, state)

    def send(step):
        for index, place in peers:
            pltpu.make_async_remote_copy(
                src_ref=packed.at[step, index], dst_ref=own.at[step, me],
                send_sem=send_sem, recv_sem=recv_sem.at[step], device_id=place, device_id_type=MESH,
            ).start()
        pltpu.make_async_copy(packed.at[step, me], own.at[step, me], recv_sem.at[step]).start()

    def pass_on(step):
        wait_bytes(own.at[step], recv_sem.at[step])
        pltpu.make_async_remote_copy(
            src_ref=own.at[step, :, 16:32, :], dst_ref=int_z.at[step],
            send_sem=zsend_sem, recv_sem=zrecv_sem.at[1, step], device_id=int_peer, device_id_type=MESH,
        ).start()
        pltpu.make_async_remote_copy(
            src_ref=own.at[step, :, 0:16, :], dst_ref=amp_z.at[step],
            send_sem=zsend_sem, recv_sem=zrecv_sem.at[0, step], device_id=amp_peer, device_id_type=MESH,
        ).start()
        pltpu.make_async_remote_copy(
            src_ref=own.at[step, :, 16:32, :], dst_ref=near.at[step, 0],
            send_sem=nsend_sem, recv_sem=nrecv_sem.at[0, step], device_id=near_peer, device_id_type=MESH,
        ).start()

    def relay(step):
        wait_bytes(int_z.at[step], zrecv_sem.at[1, step])
        pltpu.make_async_remote_copy(
            src_ref=int_z.at[step], dst_ref=near.at[step, 1],
            send_sem=nsend_sem, recv_sem=nrecv_sem.at[1, step], device_id=near_peer, device_id_type=MESH,
        ).start()

    def arrive(step):
        wait_bytes(amp_z.at[step], zrecv_sem.at[0, step])
        wait_bytes(near.at[step, 0], nrecv_sem.at[0, step])
        wait_bytes(near.at[step, 1], nrecv_sem.at[1, step])

    def multiply(step, which):
        rows = GROUP * 16
        lhs = (amp_z[step] if which else own[step, :, 0:16, :]).reshape(rows, columns)
        for n in range(NX):
            at = slice(NY * n, NY * (n + 1))
            rhs = jnp.concatenate([
                own[step, at, 16:32, :].reshape(64, columns), int_z[step, at].reshape(64, columns),
                near[step, 0, at].reshape(64, columns), near[step, 1, at].reshape(64, columns),
            ], axis=0)
            term = lax.dot_general(lhs, rhs, (((1,), (1,)), ((), ())), preferred_element_type=jnp.float32)
            total[n, which] += term.reshape(NX, NY, 16, 256)

    state = pack(0, (jnp.int32(0), jnp.int32(0)))
    pl.semaphore_wait(barrier, len(everyone))
    send(0)
    for step in range(1, ahead):
        state = pack(step, state)
        send(step)

    def behind(step):
        @pl.when(step > 0)
        def _():
            relay(step - 1)

        @pl.when(step > 1)
        def _():
            arrive(step - 2)
            multiply(step - 2, 1)
            multiply(step - 2, 0)

    def turn(step, state):
        pass_on(step)
        state = pack(step + ahead, state)
        send(step + ahead)
        behind(step)
        return state

    lax.fori_loop(0, steps - ahead, turn, state)

    def late(step, carry):
        pass_on(step)
        behind(step)
        return carry

    lax.fori_loop(steps - ahead, steps, late, 0)
    relay(steps - 1)
    arrive(steps - 2)
    multiply(steps - 2, 1)
    multiply(steps - 2, 0)
    arrive(steps - 1)

    def scatter_first(which):
        for d in (1, 2, 3):
            px, py = lax.rem(x + d, NX), lax.rem(y + d, NY)
            pltpu.make_async_remote_copy(
                src_ref=total.at[0:2, which, px], dst_ref=part_x.at[which, d - 1],
                send_sem=rsend_sem.at[0, which], recv_sem=rrecv_sem.at[0, which],
                device_id=device(px, c, y, z), device_id_type=MESH,
            ).start()
            pltpu.make_async_remote_copy(
                src_ref=total.at[2:4, which, :, py], dst_ref=part_y.at[which, d - 1],
                send_sem=rsend_sem.at[1, which], recv_sem=rrecv_sem.at[1, which],
                device_id=device(x, c, py, z), device_id_type=MESH,
            ).start()

    def scatter_second(which):
        wait_bytes(part_x.at[which], rrecv_sem.at[0, which])
        sum_x[which] = total[0:2, which, x] + part_x[which, 0] + part_x[which, 1] + part_x[which, 2]
        for d in (1, 2, 3):
            py = lax.rem(y + d, NY)
            pltpu.make_async_remote_copy(
                src_ref=sum_x.at[which, :, py], dst_ref=end_y.at[which, d - 1],
                send_sem=rsend_sem.at[2, which], recv_sem=rrecv_sem.at[2, which],
                device_id=device(x, c, py, z), device_id_type=MESH,
            ).start()
        wait_bytes(part_y.at[which], rrecv_sem.at[1, which])
        sum_y[which] = total[2:4, which, :, y] + part_y[which, 0] + part_y[which, 1] + part_y[which, 2]
        for d in (1, 2, 3):
            px = lax.rem(x + d, NX)
            pltpu.make_async_remote_copy(
                src_ref=sum_y.at[which, :, px], dst_ref=end_x.at[which, d - 1],
                send_sem=rsend_sem.at[3, which], recv_sem=rrecv_sem.at[3, which],
                device_id=device(px, c, y, z), device_id_type=MESH,
            ).start()

    def finish(which):
        wait_bytes(end_y.at[which], rrecv_sem.at[2, which])
        done[which, 0:2] = sum_x[which, :, y] + end_y[which, 0] + end_y[which, 1] + end_y[which, 2]
        wait_bytes(end_x.at[which], rrecv_sem.at[3, which])
        done[which, 2:4] = sum_y[which, :, x] + end_x[which, 0] + end_x[which, 1] + end_x[which, 2]

    def place(values, n, swap, upper):
        for j in range(2):
            piece = values[:, j * BW:(j + 1) * BW]
            piece = jnp.where(swap == 1, pltpu.roll(piece, BW // 2, 1), piece)
            core = c if j == 0 else 1 - c
            start = pl.multiple_of((2 * n + core) * 2 * BW + upper * BW, BW)
            out_ref[:, pl.ds(start, BW)] = piece

    odd, high = lax.rem(z, 2), z // 2
    multiply(steps - 1, 1)
    scatter_first(1)
    multiply(steps - 1, 0)
    scatter_first(0)
    scatter_second(1)
    finish(1)
    copy = pltpu.make_async_remote_copy(
        src_ref=done.at[1], dst_ref=other, send_sem=last_sem.at[0], recv_sem=last_sem.at[1],
        device_id=amp_peer, device_id_type=MESH,
    )
    copy.start()
    scatter_second(0)
    copy.wait()
    for n in range(NX):
        place(other[n], n, 1 - odd, 1 - high)
    finish(0)
    for n in range(NX):
        place(done[0, n], n, odd, high)

    for which in range(2):
        wait_bytes(part_x.at[which], rsend_sem.at[0, which])
        wait_bytes(part_y.at[which], rsend_sem.at[1, which])
        wait_bytes(end_y.at[which], rsend_sem.at[2, which])
        wait_bytes(end_x.at[which], rsend_sem.at[3, which])
    wait_bytes(packed.at[:, 0:GROUP - 1], send_sem)
    wait_bytes(own, zsend_sem)
    wait_bytes(near, nsend_sem)


def solution(mesh):
    steps, ahead = 32, 4

    def shards(integrals, amplitudes, block_lists):
        columns = LISTED * BW // GROUP // steps
        f32, bf16 = jnp.float32, jnp.bfloat16
        return pl.pallas_call(
            functools.partial(kernel, steps, ahead),
            out_shape=jax.ShapeDtypeStruct((16, 2048), f32),
            in_specs=[
                pl.BlockSpec(memory_space=pltpu.SMEM),
                pl.BlockSpec(memory_space=pl.ANY),
                pl.BlockSpec(memory_space=pl.ANY),
            ],
            out_specs=pl.BlockSpec(memory_space=pltpu.VMEM),
            scratch_shapes=[
                pltpu.VMEM(amplitudes.shape, bf16),
                pltpu.VMEM(integrals.shape, bf16),
                pltpu.VMEM((steps, GROUP, 32, columns), bf16),
                pltpu.VMEM((steps, GROUP, 32, columns), bf16),
                pltpu.VMEM((steps, GROUP, 16, columns), bf16),
                pltpu.VMEM((steps, GROUP, 16, columns), bf16),
                pltpu.VMEM((steps, 2, GROUP, 16, columns), bf16),
                pltpu.VMEM((NX, 2, NX, NY, 16, 256), f32),
                pltpu.VMEM((2, 3, 2, NY, 16, 256), f32),
                pltpu.VMEM((2, 3, 2, NX, 16, 256), f32),
                pltpu.VMEM((2, 2, NY, 16, 256), f32),
                pltpu.VMEM((2, 2, NX, 16, 256), f32),
                pltpu.VMEM((2, 3, 2, 16, 256), f32),
                pltpu.VMEM((2, 3, 2, 16, 256), f32),
                pltpu.VMEM((2, NX, 16, 256), f32),
                pltpu.VMEM((NX, 16, 256), f32),
                pltpu.SemaphoreType.DMA((2,)),
                pltpu.SemaphoreType.DMA,
                pltpu.SemaphoreType.DMA((steps,)),
                pltpu.SemaphoreType.DMA,
                pltpu.SemaphoreType.DMA((2, steps)),
                pltpu.SemaphoreType.DMA,
                pltpu.SemaphoreType.DMA((2, steps)),
                pltpu.SemaphoreType.DMA((4, 2)),
                pltpu.SemaphoreType.DMA((4, 2)),
                pltpu.SemaphoreType.DMA((2,)),
            ],
            compiler_params=pltpu.CompilerParams(
                collective_id=0, has_side_effects=True, vmem_limit_bytes=62 * MIB
            ),
            name="ladder",
        )(block_lists.T, amplitudes, integrals)

    return jax.shard_map(
        shards,
        mesh=mesh,
        in_specs=(P(("vc", "vd"), None), P(("vc", "vd"), None), P()),
        out_specs=P(("vc", "vd"), None),
        check_vma=False,
    )
```

time: 153 us -> 135 us (0.88)
  Pallas kernels: 149 us -> 133 us
    pallas_call x1, Pallas kernels: 142 us -> 133 us  [shards(): pl.pallas_call(functools.partial(kernel, steps, ahead), out_shape=jax.Sha...]
    pallas_call x1 -> x0, Pallas kernels: 6.84 us -> none  [shards(): pl.pallas_call(list_blocks, out_shape=jax.ShapeDtypeStruct((LISTED + 16,)...]
where the time goes in v2:
time: 135 us; the launch traced here: 134 us
  Pallas kernels  133 us (99%)
  local copies, waits for them, and re-layouts  1.57 us (1%)
    pallas_call x1, Pallas kernels, shards(): pl.pallas_call(functools.partial(kernel, steps, ahead), out_shape=jax.Sha...  133 us

profile of v2, /device:TPU:0, one launch (start us, length us, event | category | flops | bytes accessed | tf_op | source)
XLA Modules:
  0.0 134.4 jit_solution(2784351052100151770)
XLA Ops:
  0.0 132.9 %ladder.1 = f32[16,2048]{1,0:T(8,128)} custom-call(s32[15,128]{1,0:T(8,128)} %bitcast.1, bf16[16,262144]{1,0:T(8,128)(2,1)} %amp_hbm.1, bf16[16,262144]{1,0:T(8,128)(2,1)} %int_hbm.1), custom_call_target="tpu_custom_call" | custom-call | tf_op jit(solution)/shard_map/ladder/pallas_call | solution.py:247
  132.9 1.6 %copy.5 = f32[16,2048]{1,0:T(8,128)} copy(f32[16,2048]{1,0:T(8,128)} %ladder.1) | data formatting | bytes 262144

commit v3 on v2

v3 whole, which is shorter than its diff:
```python
import functools
import random

import jax
import jax.numpy as jnp
from jax import lax
from jax.experimental import pallas as pl
from jax.experimental.pallas import tpu as pltpu
from jax.sharding import PartitionSpec as P

MESH = pl.DeviceIdType.MESH
BW = 128
NX, NC, NY, NZ = 4, 2, 4, 4
GROUP = NX * NY
LISTED = 1024
MIB = 1 << 20


def device(x, c, y, z):
    return (x * NC + c, z * NY + y)


def wait_bytes(ref, sem):
    pltpu.make_async_copy(ref, ref, sem).wait()


def kernel(
    steps, ahead, lists, amp_hbm, int_hbm, out_ref,
    amp, integ, packed, own, amp_z, int_z, near, total, part_x, part_y, sum_x, sum_y, end_y, end_x, done,
    load_sem, send_sem, recv_sem, zsend_sem, zrecv_sem, nsend_sem, nrecv_sem, rsend_sem, rrecv_sem,
):
    vc, vd = lax.axis_index("vc"), lax.axis_index("vd")
    x, c, z, y = vc // NC, lax.rem(vc, NC), vd // NY, lax.rem(vd, NY)
    me = x * NY + y
    amp_peer = device(x, c, y, 3 - z)
    int_peer = device(x, c, y, z + 1 - 2 * lax.rem(z, 2))
    near_peer = device(x, 1 - c, y, z)
    order = [(dx, dy) for dx in range(NX) for dy in range(NY)][1:]
    random.Random(1).shuffle(order)
    peers = []
    for dx, dy in order:
        px, py = lax.rem(x + dx, NX), lax.rem(y + dy, NY)
        peers.append((px * NY + py, device(px, c, py, z)))
    columns = packed.shape[3]
    blocks = columns // BW
    slots, owners = lists.shape

    loads = [
        pltpu.make_async_copy(amp_hbm, amp, load_sem.at[0]),
        pltpu.make_async_copy(int_hbm, integ, load_sem.at[1]),
    ]
    for load in loads:
        load.start()
    barrier = pltpu.get_barrier_semaphore()
    across = [device(x, c, lax.rem(y + d, NY), 3 - z) for d in (1, 2, 3)]
    across += [device(lax.rem(x + d, NX), c, y, 3 - z) for d in (1, 2, 3)]
    everyone = [place for _, place in peers] + across + [amp_peer, int_peer, near_peer]
    for place in everyone:
        pl.semaphore_signal(barrier, inc=1, device_id=place, device_id_type=MESH)
    total[...] = jnp.zeros_like(total)
    for load in loads:
        load.wait()

    def pack(step, state):
        def one(member, state):
            owner, slot = state
            for block in range(blocks):
                start = lists[slot, owner] * BW
                packed[step, member, 0:16, block * BW:(block + 1) * BW] = amp[:, pl.ds(start, BW)]
                packed[step, member, 16:32, block * BW:(block + 1) * BW] = integ[:, pl.ds(start, BW)]
                following = lists[jnp.minimum(slot + 1, slots - 1), owner]
                stays = jnp.logical_and(slot + 1 < slots, following >= 0)
                slot = jnp.where(stays, slot + 1, 0)
                owner = jnp.minimum(jnp.where(stays, owner, owner + 1), owners - 1)
            return owner, slot

        return lax.fori_loop(0, GROUP, one, state)

    def send(step):
        for index, place in peers:
            pltpu.make_async_remote_copy(
                src_ref=packed.at[step, index], dst_ref=own.at[step, me],
                send_sem=send_sem, recv_sem=recv_sem.at[step], device_id=place, device_id_type=MESH,
            ).start()
        pltpu.make_async_copy(packed.at[step, me], own.at[step, me], recv_sem.at[step]).start()

    def pass_on(step):
        wait_bytes(own.at[step], recv_sem.at[step])
        pltpu.make_async_remote_copy(
            src_ref=own.at[step, :, 16:32, :], dst_ref=int_z.at[step],
            send_sem=zsend_sem, recv_sem=zrecv_sem.at[1, step], device_id=int_peer, device_id_type=MESH,
        ).start()
        pltpu.make_async_remote_copy(
            src_ref=own.at[step, :, 0:16, :], dst_ref=amp_z.at[step],
            send_sem=zsend_sem, recv_sem=zrecv_sem.at[0, step], device_id=amp_peer, device_id_type=MESH,
        ).start()
        pltpu.make_async_remote_copy(
            src_ref=own.at[step, :, 16:32, :], dst_ref=near.at[step, 0],
            send_sem=nsend_sem, recv_sem=nrecv_sem.at[0, step], device_id=near_peer, device_id_type=MESH,
        ).start()

    def relay(step):
        wait_bytes(int_z.at[step], zrecv_sem.at[1, step])
        pltpu.make_async_remote_copy(
            src_ref=int_z.at[step], dst_ref=near.at[step, 1],
            send_sem=nsend_sem, recv_sem=nrecv_sem.at[1, step], device_id=near_peer, device_id_type=MESH,
        ).start()

    def multiply(step, row, col):
        rows = GROUP * 16
        lhs = (amp_z[step] if row else own[step, :, 0:16, :]).reshape(rows, columns)
        for pair in range(NX // 2):
            pieces = []
            for n in (2 * pair, 2 * pair + 1):
                at = slice(NY * n, NY * (n + 1))
                pieces.append((int_z[step, at] if col else own[step, at, 16:32, :]).reshape(64, columns))
                pieces.append(near[step, col, at].reshape(64, columns))
            rhs = jnp.concatenate(pieces, axis=0)
            term = lax.dot_general(lhs, rhs, (((1,), (1,)), ((), ())), preferred_element_type=jnp.float32)
            for i in range(2):
                part = term[:, i * BW:(i + 1) * BW].reshape(NX, NY, 16, BW)
                if pair == 0:
                    total[row, col, 0, :, i] += part
                else:
                    for k in range(NX):
                        total[row, col, 1, :, i, k] += part[k]

    def arrive_rows(step):
        wait_bytes(amp_z.at[step], zrecv_sem.at[0, step])

    def arrive_near(step, col):
        wait_bytes(near.at[step, col], nrecv_sem.at[col, step])

    state = pack(0, (jnp.int32(0), jnp.int32(0)))
    pl.semaphore_wait(barrier, len(everyone))
    send(0)
    for step in range(1, ahead):
        state = pack(step, state)
        send(step)

    def behind(step):
        @pl.when(step > 0)
        def _():
            relay(step - 1)

        @pl.when(step > 1)
        def _():
            arrive_near(step - 2, 0)
            arrive_rows(step - 2)
            arrive_near(step - 2, 1)
            for row in range(2):
                for col in range(2):
                    multiply(step - 2, row, col)

    def turn(step, state):
        pass_on(step)
        state = pack(step + ahead, state)
        send(step + ahead)
        behind(step)
        return state

    lax.fori_loop(0, steps - ahead, turn, state)

    def late(step, carry):
        pass_on(step)
        behind(step)
        return carry

    lax.fori_loop(steps - ahead, steps, late, 0)

    def scatter_first(row, col):
        q = 2 * row + col
        for d in (1, 2, 3):
            px, py = lax.rem(x + d, NX), lax.rem(y + d, NY)
            pltpu.make_async_remote_copy(
                src_ref=total.at[row, col, 0, px], dst_ref=part_x.at[q, d - 1],
                send_sem=rsend_sem.at[0, q], recv_sem=rrecv_sem.at[0, q],
                device_id=device(px, c, y, z), device_id_type=MESH,
            ).start()
            pltpu.make_async_remote_copy(
                src_ref=total.at[row, col, 1, py], dst_ref=part_y.at[q, d - 1],
                send_sem=rsend_sem.at[1, q], recv_sem=rrecv_sem.at[1, q],
                device_id=device(x, c, py, z), device_id_type=MESH,
            ).start()

    def scatter_second(row, col):
        q = 2 * row + col
        wait_bytes(part_x.at[q], rrecv_sem.at[0, q])
        for i in range(2):
            sum_x[q, :, i] = total[row, col, 0, x, i] + part_x[q, 0, i] + part_x[q, 1, i] + part_x[q, 2, i]
        for d in range(1 - row, 4):
            py = lax.rem(y + d, NY)
            pltpu.make_async_remote_copy(
                src_ref=sum_x.at[q, py], dst_ref=end_y.at[q, d],
                send_sem=rsend_sem.at[2, q], recv_sem=rrecv_sem.at[2, q],
                device_id=device(x, c, py, 3 - z if row else z), device_id_type=MESH,
            ).start()
        wait_bytes(part_y.at[q], rrecv_sem.at[1, q])
        for i in range(2):
            sum_y[q, :, i] = total[row, col, 1, y, i] + part_y[q, 0, i] + part_y[q, 1, i] + part_y[q, 2, i]
        for d in range(1 - row, 4):
            px = lax.rem(x + d, NX)
            pltpu.make_async_remote_copy(
                src_ref=sum_y.at[q, px], dst_ref=end_x.at[q, d],
                send_sem=rsend_sem.at[3, q], recv_sem=rrecv_sem.at[3, q],
                device_id=device(px, c, y, 3 - z if row else z), device_id_type=MESH,
            ).start()

    def finish(row, col):
        q = 2 * row + col
        wait_bytes(end_y.at[q, 1 - row:4], rrecv_sem.at[2, q])
        mine = end_y[q, 0] if row else sum_x[q, y]
        done[q, 0:2] = mine + end_y[q, 1] + end_y[q, 2] + end_y[q, 3]
        wait_bytes(end_x.at[q, 1 - row:4], rrecv_sem.at[3, q])
        mine = end_x[q, 0] if row else sum_y[q, x]
        done[q, 2:4] = mine + end_x[q, 1] + end_x[q, 2] + end_x[q, 3]

    def place(own_part, partner_part, odd, upper):
        lower_lanes = lax.broadcasted_iota(jnp.int32, (16, BW), 1) < BW // 2
        for n in range(NX):
            first = jnp.where(odd == 1, partner_part[n], own_part[n])
            second = jnp.where(odd == 1, own_part[n], partner_part[n])
            pieces = (
                jnp.where(lower_lanes, first, pltpu.roll(second, BW // 2, 1)),
                jnp.where(lower_lanes, pltpu.roll(first, BW // 2, 1), second),
            )
            for core, piece in zip((c, 1 - c), pieces):
                start = pl.multiple_of((2 * n + core) * 2 * BW + upper * BW, BW)
                out_ref[:, pl.ds(start, BW)] = piece

    for step in (steps - 2, steps - 1):
        arrive_near(step, 0)
        multiply(step, 0, 0)
    scatter_first(0, 0)
    relay(steps - 1)
    arrive_rows(steps - 2)
    multiply(steps - 2, 1, 0)
    arrive_near(steps - 2, 1)
    multiply(steps - 2, 1, 1)
    multiply(steps - 2, 0, 1)
    arrive_rows(steps - 1)
    multiply(steps - 1, 1, 0)
    scatter_first(1, 0)
    scatter_second(0, 0)
    arrive_near(steps - 1, 1)
    multiply(steps - 1, 1, 1)
    scatter_first(1, 1)
    multiply(steps - 1, 0, 1)
    scatter_second(1, 0)
    scatter_first(0, 1)
    finish(0, 0)
    scatter_second(1, 1)
    finish(1, 0)
    scatter_second(0, 1)
    finish(1, 1)
    finish(0, 1)
    odd, high = lax.rem(z, 2), z // 2
    place(done.at[0], done.at[1], odd, high)
    place(done.at[2], done.at[3], 1 - odd, 1 - high)

    for q in range(4):
        wait_bytes(part_x.at[q], rsend_sem.at[0, q])
        wait_bytes(part_y.at[q], rsend_sem.at[1, q])
        wait_bytes(end_y.at[q, 1 - q // 2:4], rsend_sem.at[2, q])
        wait_bytes(end_x.at[q, 1 - q // 2:4], rsend_sem.at[3, q])
    wait_bytes(packed.at[:, 0:GROUP - 1], send_sem)
    wait_bytes(own, zsend_sem)
    wait_bytes(near, nsend_sem)


def solution(mesh):
    steps, ahead = 32, 4

    def shards(integrals, amplitudes, block_lists):
        columns = LISTED * BW // GROUP // steps
        f32, bf16 = jnp.float32, jnp.bfloat16
        return pl.pallas_call(
            functools.partial(kernel, steps, ahead),
            out_shape=jax.ShapeDtypeStruct((16, 2048), f32),
            in_specs=[
                pl.BlockSpec(memory_space=pltpu.SMEM),
                pl.BlockSpec(memory_space=pl.ANY),
                pl.BlockSpec(memory_space=pl.ANY),
            ],
            out_specs=pl.BlockSpec(memory_space=pltpu.VMEM),
            scratch_shapes=[
                pltpu.VMEM(amplitudes.shape, bf16),
                pltpu.VMEM(integrals.shape, bf16),
                pltpu.VMEM((steps, GROUP, 32, columns), bf16),
                pltpu.VMEM((steps, GROUP, 32, columns), bf16),
                pltpu.VMEM((steps, GROUP, 16, columns), bf16),
                pltpu.VMEM((steps, GROUP, 16, columns), bf16),
                pltpu.VMEM((steps, 2, GROUP, 16, columns), bf16),
                pltpu.VMEM((2, 2, 2, NX, 2, NY, 16, BW), f32),
                pltpu.VMEM((4, 3, 2, NY, 16, BW), f32),
                pltpu.VMEM((4, 3, 2, NX, 16, BW), f32),
                pltpu.VMEM((4, NY, 2, 16, BW), f32),
                pltpu.VMEM((4, NX, 2, 16, BW), f32),
                pltpu.VMEM((4, 4, 2, 16, BW), f32),
                pltpu.VMEM((4, 4, 2, 16, BW), f32),
                pltpu.VMEM((4, NX, 16, BW), f32),
                pltpu.SemaphoreType.DMA((2,)),
                pltpu.SemaphoreType.DMA,
                pltpu.SemaphoreType.DMA((steps,)),
                pltpu.SemaphoreType.DMA,
                pltpu.SemaphoreType.DMA((2, steps)),
                pltpu.SemaphoreType.DMA,
                pltpu.SemaphoreType.DMA((2, steps)),
                pltpu.SemaphoreType.DMA((4, 4)),
                pltpu.SemaphoreType.DMA((4, 4)),
            ],
            compiler_params=pltpu.CompilerParams(
                collective_id=0, has_side_effects=True, vmem_limit_bytes=62 * MIB
            ),
            name="ladder",
        )(block_lists.T, amplitudes, integrals)

    return jax.shard_map(
        shards,
        mesh=mesh,
        in_specs=(P(("vc", "vd"), None), P(("vc", "vd"), None), P()),
        out_specs=P(("vc", "vd"), None),
        check_vma=False,
    )
```

time: 135 us -> 132 us (0.978)
  Pallas kernels: 133 us -> 130 us
    pallas_call x1, Pallas kernels: 133 us -> 130 us  [shards(): pl.pallas_call(functools.partial(kernel, steps, ahead), out_shape=jax.Sha...]
where the time goes in v3:
time: 132 us; the launch traced here: 131 us
  Pallas kernels  130 us (98%)
  local copies, waits for them, and re-layouts  1.57 us (1%)
    pallas_call x1, Pallas kernels, shards(): pl.pallas_call(functools.partial(kernel, steps, ahead), out_shape=jax.Sha...  130 us

profile of v3, /device:TPU:0, one launch (start us, length us, event | category | flops | bytes accessed | tf_op | source)
XLA Modules:
  0.0 131.5 jit_solution(13942611271198472987)
XLA Ops:
  0.0 129.9 %ladder.1 = f32[16,2048]{1,0:T(8,128)} custom-call(s32[15,128]{1,0:T(8,128)} %bitcast.1, bf16[16,262144]{1,0:T(8,128)(2,1)} %amp_hbm.1, bf16[16,262144]{1,0:T(8,128)(2,1)} %int_hbm.1), custom_call_target="tpu_custom_call" | custom-call | tf_op jit(solution)/shard_map/ladder/pallas_call | solution.py:277
  129.9 1.6 %copy.5 = f32[16,2048]{1,0:T(8,128)} copy(f32[16,2048]{1,0:T(8,128)} %ladder.1) | data formatting | bytes 262144

commit v4 on v3

--- a/solution.py
+++ b/solution.py
@@ -25,7 +25,7 @@
 
 
 def kernel(
-    steps, ahead, lists, amp_hbm, int_hbm, out_ref,
+    steps, ahead, relay_lag, lag, lists, amp_hbm, int_hbm, out_ref,
     amp, integ, packed, own, amp_z, int_z, near, total, part_x, part_y, sum_x, sum_y, end_y, end_x, done,
     load_sem, send_sem, recv_sem, zsend_sem, zrecv_sem, nsend_sem, nrecv_sem, rsend_sem, rrecv_sem,
 ):
@@ -138,19 +138,26 @@
         state = pack(step, state)
         send(step)
 
+    def settle(step):
+        arrive_rows(step)
+        arrive_near(step, 1)
+        multiply(step, 1, 0)
+        multiply(step, 1, 1)
+        multiply(step, 0, 1)
+
     def behind(step):
-        @pl.when(step > 0)
+        @pl.when(step >= relay_lag)
         def _():
-            relay(step - 1)
-
-        @pl.when(step > 1)
+            relay(step - relay_lag)
+
+        @pl.when(step >= lag)
         def _():
-            arrive_near(step - 2, 0)
-            arrive_rows(step - 2)
-            arrive_near(step - 2, 1)
+            arrive_near(step - lag, 0)
+            arrive_rows(step - lag)
+            arrive_near(step - lag, 1)
             for row in range(2):
                 for col in range(2):
-                    multiply(step - 2, row, col)
+                    multiply(step - lag, row, col)
 
     def turn(step, state):
         pass_on(step)
@@ -170,7 +177,7 @@
 
     def scatter_first(row, col):
         q = 2 * row + col
-        for d in (1, 2, 3):
+        for d in (2, 1, 3):
             px, py = lax.rem(x + d, NX), lax.rem(y + d, NY)
             pltpu.make_async_remote_copy(
                 src_ref=total.at[row, col, 0, px], dst_ref=part_x.at[q, d - 1],
@@ -228,16 +235,17 @@
                 start = pl.multiple_of((2 * n + core) * 2 * BW + upper * BW, BW)
                 out_ref[:, pl.ds(start, BW)] = piece
 
-    for step in (steps - 2, steps - 1):
+    for step in range(steps - relay_lag, steps - 2):
+        relay(step)
+    for step in range(steps - lag, steps):
         arrive_near(step, 0)
         multiply(step, 0, 0)
     scatter_first(0, 0)
+    if relay_lag > 1:
+        relay(steps - 2)
+    for step in range(steps - lag, steps - 1):
+        settle(step)
     relay(steps - 1)
-    arrive_rows(steps - 2)
-    multiply(steps - 2, 1, 0)
-    arrive_near(steps - 2, 1)
-    multiply(steps - 2, 1, 1)
-    multiply(steps - 2, 0, 1)
     arrive_rows(steps - 1)
     multiply(steps - 1, 1, 0)
     scatter_first(1, 0)
@@ -250,13 +258,13 @@
     scatter_first(0, 1)
     finish(0, 0)
     scatter_second(1, 1)
+    scatter_second(0, 1)
+    odd, high = lax.rem(z, 2), z // 2
     finish(1, 0)
-    scatter_second(0, 1)
     finish(1, 1)
+    place(done.at[2], done.at[3], 1 - odd, 1 - high)
     finish(0, 1)
-    odd, high = lax.rem(z, 2), z // 2
     place(done.at[0], done.at[1], odd, high)
-    place(done.at[2], done.at[3], 1 - odd, 1 - high)
 
     for q in range(4):
         wait_bytes(part_x.at[q], rsend_sem.at[0, q])
@@ -269,13 +277,13 @@
 
 
 def solution(mesh):
-    steps, ahead = 32, 4
+    steps, ahead, relay_lag, lag = 32, 6, 2, 4
 
     def shards(integrals, amplitudes, block_lists):
         columns = LISTED * BW // GROUP // steps
         f32, bf16 = jnp.float32, jnp.bfloat16
         return pl.pallas_call(
-            functools.partial(kernel, steps, ahead),
+            functools.partial(kernel, steps, ahead, relay_lag, lag),
             out_shape=jax.ShapeDtypeStruct((16, 2048), f32),
             in_specs=[
                 pl.BlockSpec(memory_space=pltpu.SMEM),

time: 132 us -> 131 us (level)
  no operation moved by 1% of the time
where the time goes in v4:
time: 131 us
  Pallas kernels  129 us (98%)
  local copies, waits for them, and re-layouts  1.57 us (1%)
    pallas_call x1, Pallas kernels, shards(): pl.pallas_call(functools.partial(kernel, steps, ahead, relay_lag, lag), o...  129 us

profile of v4, /device:TPU:0, one launch (start us, length us, event | category | flops | bytes accessed | tf_op | source)
XLA Modules:
  0.0 130.6 jit_solution(4772196540707385459)
XLA Ops:
  0.0 129.0 %ladder.1 = f32[16,2048]{1,0:T(8,128)} custom-call(s32[15,128]{1,0:T(8,128)} %bitcast.1, bf16[16,262144]{1,0:T(8,128)(2,1)} %amp_hbm.1, bf16[16,262144]{1,0:T(8,128)(2,1)} %int_hbm.1), custom_call_target="tpu_custom_call" | custom-call | tf_op jit(solution)/shard_map/ladder/pallas_call | solution.py:285
  129.0 1.6 %copy.5 = f32[16,2048]{1,0:T(8,128)} copy(f32[16,2048]{1,0:T(8,128)} %ladder.1) | data formatting | bytes 262144
